TPU v7x, 256 devices: a whole 4x4x8 slice. The times are simulated.
256 devices in a mesh: param: 4 (over y_lo, core), tile: 64 (over x, y_hi, z).
Axes of the slice: x: 4, y: 4 (y_hi: 2, y_lo: 2; y = y_hi * 2 + y_lo), z: 8, core: 2. Of those that a mesh axis runs over, the one named last changes fastest.
Arguments:
- concentration: float32 [160, 4, 8192], P(None, 'param', 'tile'), may hold values from 0.05 to 3
- reaction_rates: float32 [160, 4, 8192], P(None, None, 'tile'), may hold values from 0.4 to 0.8
- coupling: bfloat16 [160, 160], replicated, may hold values from -0.5 to 0.5
- profile: float32 [16, 160], replicated, may hold values from 0.05 to 0.5
- source_field: float32 [16, 4, 8192], P(None, None, 'tile'), may hold values from 0.1 to 1
- source_map: int32 [64], P('param'), may hold values from 0 to 15
- param_weight: float32 [64], P('param'), may hold values from 0.5 to 2
- sensitivity: bfloat16 [64, 160, 4, 8192], P('param', None, None, 'tile'), may hold values from -6 to 6
- courant: float32 [4, 4, 8192], P(None, None, 'tile'), may hold values from -0.25 to 0.25, as said below
Outputs:
- state_next: float32 [160, 4, 8192], P(None, 'param', 'tile')
- sensitivity_next: bfloat16 [64, 160, 4, 8192], P('param', None, None, 'tile')
Inputs may be any that keep to these rules, and one draw needn't show every extreme that they name: `courant`: A cell's east value equals the west value of the next row's cell in the same column, and its north value the south value of the next column's cell in the same row; positive values point toward larger indices.
All inputs are finite; a program needn't handle non-finite values.
Results may differ from a plain program's by a relative error of at most 0.0048.
Values may be sent and summed in bfloat16 or wider, within the bound.
A program may use at most 128 MiB of HBM per device.

v0:
```python
import math
from functools import partial

import jax
import jax.numpy as jnp
from jax import lax
from jax.experimental import pallas as pl
from jax.experimental.pallas import tpu as pltpu
from jax.sharding import PartitionSpec as P

ITERS = 3
NY = 64
LANES = 128
STRAIGHT = 2
AHEAD = 2
READY = STRAIGHT + AHEAD
DEPTH = 8
WIRE = jnp.bfloat16
GROUP = 2
MESH = pl.DeviceIdType.MESH

section_gamma = 1.0 + 1.0 / math.sqrt(2.0)


def series():
    q = [section_gamma**k for k in range(ITERS + 1)]
    square = [0.0] * (2 * ITERS + 2)
    for i, left in enumerate(q):
        for j, right in enumerate(q):
            square[i + j] += left * right
    c = [-value for value in square]
    for k, value in enumerate(q):
        c[k] += 2.0 * value
    for k in range(2 * ITERS + 1):
        c[k + 1] += 0.5 * square[k]
    return c


COEFFS = series()


def rolled(x, shift):
    return pltpu.roll(x, shift, 1)


def face_factors(rows, lane, has_west, has_east):
    west, east, south, north = rows
    column = lane % NY
    first = lane < NY
    plus = [jnp.maximum(face, 0.0) for face in rows]
    minus = [jnp.minimum(face, 0.0) for face in rows]
    own = 1.0 + minus[0] - plus[1] + minus[2] - plus[3]
    from_south = jnp.where(column == 0, 0.0, plus[2])
    from_north = jnp.where(column == NY - 1, 0.0, -minus[3])
    across = jnp.where(first, -minus[1], plus[0])
    halo = jnp.where(first, plus[0] * has_west, -minus[1] * has_east)
    return own, from_south, from_north, across, halo


def inner(q, factors):
    own, from_south, from_north, across, _ = factors
    return (
        own * q
        + from_south * rolled(q, 1)
        + from_north * rolled(q, LANES - 1)
        + across * rolled(q, NY)
    )


def kernel(
    tiles,
    params,
    conc_ref,
    rates_ref,
    coupling_ref,
    profile_ref,
    field_ref,
    courant_ref,
    map_ref,
    weight_ref,
    sens_ref,
    state_ref,
    next_ref,
    sens,
    adv,
    east_out,
    west_out,
    east_in,
    west_in,
    relay,
    conc_east_out,
    conc_west_out,
    conc_east_in,
    conc_west_in,
    damping,
    wire,
    rates,
    factors_dw,
    spread,
    work,
    result,
    load_sem,
    store_sem,
    east_send,
    east_recv,
    west_send,
    west_recv,
    conc_send,
    conc_recv,
    damp_send,
    damp_recv,
    relay_send,
    relay_recv,
):
    count, rows, _ = sens.shape
    species, layers = coupling_ref.shape[0], params
    half = rows // 2
    param = lax.axis_index("param")
    tile = lax.axis_index("tile")
    right = lax.rem(tile + 1, tiles)
    left = lax.rem(tile + tiles - 1, tiles)
    has_west = (tile > 0).astype(jnp.float32)
    has_east = (tile < tiles - 1).astype(jnp.float32)
    sibling = param + 1 - 2 * lax.rem(param, 2)
    across = lax.rem(param + 2, params)
    peers = [(sibling, tile), (across, tile)]

    def load(p):
        return pltpu.make_async_copy(sens_ref.at[p], sens.at[p], load_sem.at[p])

    def store(p):
        return pltpu.make_async_copy(result.at[p], next_ref.at[p], store_sem.at[p])

    def remote(src, dst, send, recv, device):
        return pltpu.make_async_remote_copy(
            src_ref=src,
            dst_ref=dst,
            send_sem=send,
            recv_sem=recv,
            device_id=device,
            device_id_type=MESH,
        )

    def send_east(p):
        return remote(
            east_out.at[p], east_in.at[p], east_send.at[p], east_recv.at[p], (param, right)
        )

    def send_west(p):
        return remote(
            west_out.at[p], west_in.at[p], west_send.at[p], west_recv.at[p], (param, left)
        )

    conc_copies = [
        remote(conc_east_out, conc_east_in, conc_send.at[0], conc_recv.at[0], (param, right)),
        remote(conc_west_out, conc_west_in, conc_send.at[1], conc_recv.at[1], (param, left)),
    ]
    damp_copies = [
        remote(wire.at[slot], wire.at[slot], damp_send.at[k], damp_recv.at[k], device)
        for k, (slot, device) in enumerate(
            [(param, (across, tile)), (param, (sibling, tile)), (across, (sibling, tile))]
        )
    ]
    has_left, has_right = tile > 0, tile < tiles - 1
    level = lax.rem(tile, DEPTH)
    top = jnp.logical_and(level == DEPTH - 1, has_right)
    bottom = jnp.logical_and(level == 0, has_left)
    via = jnp.logical_or(top, bottom)
    east_direct = jnp.logical_and(level < DEPTH - 1, has_right)
    west_direct = jnp.logical_and(level > 0, has_left)

    def relay_east(p):
        return remote(
            east_out.at[p], relay.at[p], relay_send.at[p], relay_recv.at[p], (across, tile)
        )

    def relay_west(p):
        return remote(
            west_out.at[p], relay.at[p], relay_send.at[p], relay_recv.at[p], (across, tile)
        )

    def onward_east(p):
        return remote(
            relay.at[p], east_in.at[p], east_send.at[p], east_recv.at[p], (across, right)
        )

    def onward_west(p):
        return remote(
            relay.at[p], west_in.at[p], west_send.at[p], west_recv.at[p], (across, left)
        )

    barrier = pltpu.get_barrier_semaphore()
    for device in peers:
        pl.semaphore_signal(barrier, inc=1, device_id=device, device_id_type=MESH)

    @pl.when(has_right)
    def _():
        pl.semaphore_signal(barrier, inc=1, device_id=(param, right), device_id_type=MESH)

    @pl.when(has_left)
    def _():
        pl.semaphore_signal(barrier, inc=1, device_id=(param, left), device_id_type=MESH)

    @pl.when(top)
    def _():
        pl.semaphore_signal(barrier, inc=1, device_id=(across, right), device_id_type=MESH)

    @pl.when(bottom)
    def _():
        pl.semaphore_signal(barrier, inc=1, device_id=(across, left), device_id_type=MESH)

    @pl.when(jnp.logical_not(has_left))
    def _():
        conc_east_in[...] = jnp.zeros_like(conc_east_in)
        east_in[...] = jnp.zeros_like(east_in)

    @pl.when(jnp.logical_not(has_right))
    def _():
        conc_west_in[...] = jnp.zeros_like(conc_west_in)
        west_in[...] = jnp.zeros_like(west_in)

    @pl.loop(0, count)
    def _(p):
        load(p).start()

    lane_wide = lax.broadcasted_iota(jnp.int32, (8, LANES), 1)
    lane_one = lax.broadcasted_iota(jnp.int32, (1, LANES), 1)

    def first_lanes(n):
        return lax.broadcasted_iota(jnp.int32, (n, LANES), 1) < NY

    conc = conc_ref[...]
    low, high = conc[: species // 2], conc[species // 2 :]
    turned = rolled(low, NY)
    first = first_lanes(species // 2)
    conc_east_out[...] = jnp.where(first, turned, high).astype(jnp.bfloat16)
    conc_west_out[...] = jnp.where(first, high, turned).astype(jnp.bfloat16)

    faces = [
        jnp.concatenate([courant_ref[pl.ds(layers * f, layers), :]] * (8 // layers), axis=0)
        for f in range(4)
    ]
    wide = face_factors(faces, lane_wide, has_west, has_east)
    wide = [jnp.tile(factor, (rows // 8, 1)) for factor in wide]
    select = first_lanes(half)

    def pack(p):
        load(p).wait()
        q = sens[p].astype(jnp.float32)
        q_low, q_high = q[:half], q[half:]
        across_low = rolled(q_low, NY)
        east_out[p] = jnp.where(select, across_low, q_high).astype(jnp.bfloat16)
        west_out[p] = jnp.where(select, q_high, across_low).astype(jnp.bfloat16)
        adv[p] = inner(q, wide)

    pl.loop(0, READY)(pack)

    greeted = sum(flag.astype(jnp.int32) for flag in (has_left, has_right, top, bottom))
    pl.semaphore_wait(barrier, len(peers) + greeted)

    pl.when(has_right)(conc_copies[0].start)
    pl.when(has_left)(conc_copies[1].start)

    def issue(p):
        straight = p < STRAIGHT
        pl.when(jnp.logical_and(top, p >= STRAIGHT))(lambda: relay_east(p).start())
        pl.when(jnp.logical_and(bottom, p >= STRAIGHT))(lambda: relay_west(p).start())
        pl.when(jnp.logical_or(east_direct, jnp.logical_and(top, straight)))(
            lambda: send_east(p).start()
        )
        pl.when(jnp.logical_or(west_direct, jnp.logical_and(bottom, straight)))(
            lambda: send_west(p).start()
        )

    def forward(step):
        p = step + STRAIGHT
        pl.when(jnp.logical_and(via, p + AHEAD < count))(lambda: issue(p + AHEAD))

        @pl.when(jnp.logical_and(top, p < count))
        def _():
            relay_east(p).wait_recv()
            onward_east(p).start()

        @pl.when(jnp.logical_and(bottom, p < count))
        def _():
            relay_west(p).wait_recv()
            onward_west(p).start()

    pl.loop(0, READY)(lambda step: issue(READY - 1 - step))

    @pl.loop(READY, count)
    def _(p):
        pack(p)
        pl.when(jnp.logical_not(via))(lambda: issue(p))

        @pl.when(p == count // 2)
        def _():
            forward(0)

    forward(1)

    own_faces = [courant_ref[pl.ds(layers * f + param, 1), :] for f in range(4)]
    own_factors = face_factors(own_faces, lane_one, has_west, has_east)
    pl.when(has_left)(conc_copies[0].wait_recv)
    pl.when(has_right)(conc_copies[1].wait_recv)
    east = conc_east_in[...].astype(jnp.float32)
    west = conc_west_in[...].astype(jnp.float32)
    conc_halo = jnp.concatenate(
        [jnp.where(first, east, west), rolled(jnp.where(first, west, east), NY)], axis=0
    )
    conc_adv = inner(conc, own_factors) + own_factors[4] * conc_halo
    own_tanh = jnp.tanh(conc_adv)
    own_damping = 1.0 - own_tanh * own_tanh
    wire[param] = own_damping.astype(WIRE)
    damp_copies[0].start()
    damp_copies[1].start()

    forward(2)

    coupling = coupling_ref[...]
    profile = profile_ref[...].T
    own_rates = rates_ref[pl.ds(param, species, stride=layers), :]

    for k in range(profile.shape[1]):
        spread[k] = jnp.broadcast_to(profile[:, k : k + 1], (species, LANES))

    forwarded = [3]

    def forward_next():
        forward(forwarded[0])
        forwarded[0] += 1

    def couple(x):
        top = x.astype(jnp.bfloat16)
        rest = (x - top.astype(jnp.float32)).astype(jnp.bfloat16)
        both = jnp.dot(
            coupling,
            jnp.concatenate([top, rest], axis=1),
            preferred_element_type=jnp.float32,
        )
        return both[:, :LANES] + both[:, LANES:]

    emission = jnp.zeros((species, LANES), jnp.float32)
    for k in range(profile.shape[1]):
        emission += spread[k] * field_ref[pl.ds(layers * k + param, 1), :]

    forward_next()
    damp_copies[0].wait_recv()
    damp_copies[2].start()

    own_dw = section_gamma * own_rates
    own_scaled = own_dw * own_damping

    def solve(right_side):
        scaled = own_damping * right_side
        z = scaled
        for _ in range(ITERS - 1):
            z = scaled + own_scaled * couple(z)
        return right_side + own_dw * couple(z)

    one = solve(emission + own_rates * couple(own_tanh))
    forward_next()
    two = solve(emission + own_rates * couple(jnp.tanh(conc_adv + one)) - 2.0 * one)
    forward_next()
    state_ref[...] = conc_adv + 1.5 * one + 0.5 * two

    for copy in damp_copies[1:]:
        copy.wait_recv()
    for layer in range(layers):
        rate = rates_ref[pl.ds(layer, species, stride=layers), :]
        here = wire[layer].astype(jnp.float32)
        damping[layer] = here
        rates[layer] = rate
        product = rate * here
        for k in range(1, 2 * ITERS + 1):
            factors_dw[k, layer] = (COEFFS[k + 1] / COEFFS[k]) * product
        factors_dw[0, layer] = (COEFFS[1] / COEFFS[0]) * rate

    def lanes(parts):
        return jnp.concatenate(parts, axis=1)

    def gather_edges(p, slot):
        pl.when(has_left)(send_east(p).wait_recv)
        pl.when(has_right)(send_west(p).wait_recv)

        east, west = east_in[p].astype(jnp.float32), west_in[p].astype(jnp.float32)
        here = work.at[slot]
        here[:half] = adv[p, :half] + wide[4][:half] * jnp.where(select, east, west)
        here[half:] = adv[p, half:] + wide[4][half:] * rolled(jnp.where(select, west, east), NY)
        source_index = map_ref[p]
        chosen = spread[source_index]
        field = weight_ref[p] * field_ref[pl.ds(layers * source_index, layers), :]
        a = lanes([here[pl.ds(layer, species, stride=layers), :] for layer in range(layers)])
        source = lanes([chosen * field[layer : layer + 1] for layer in range(layers)])
        return a, source

    def product(z):
        return jnp.dot(coupling, z.astype(jnp.bfloat16), preferred_element_type=jnp.float32)

    @pl.loop(0, count // GROUP)
    def _(group):
        base = group * GROUP
        members = range(GROUP)
        late = count // (2 * GROUP)
        following = forwarded[0] + group + jnp.maximum(group - late, 0)
        forward(following)
        pl.when(group >= late)(lambda: forward(following + 1))

        both = [gather_edges(base + g, g) for g in members]
        d = lanes([damping[layer] for layer in range(layers)])
        w = lanes([rates[layer] for layer in range(layers)])
        v = [w * product(d * a) + source for a, source in both]
        u = [d * value for value in v]
        z = u
        for k in range(2 * ITERS, 0, -1):
            factor = lanes([factors_dw[k, layer] for layer in range(layers)])
            z = [u[g] + factor * product(z[g]) for g in members]
        factor = lanes([factors_dw[0, layer] for layer in range(layers)])
        for g in members:
            out = both[g][0] + v[g] + factor * product(z[g])
            here = work.at[g]
            for layer in range(layers):
                here[pl.ds(layer, species, stride=layers), :] = out[
                    :, layer * LANES : (layer + 1) * LANES
                ]
            result[base + g] = here[...].astype(jnp.bfloat16)
            store(base + g).start()

    for copy in damp_copies:
        copy.wait_send()
    pl.when(has_right)(conc_copies[0].wait_send)
    pl.when(has_left)(conc_copies[1].wait_send)

    @pl.loop(0, count)
    def _(p):
        pl.when(has_right)(send_east(p).wait_send)
        pl.when(has_left)(send_west(p).wait_send)
        pl.when(jnp.logical_and(via, p >= STRAIGHT))(lambda: relay_east(p).wait_send())
        store(p).wait()


def hand_over(state_from, next_from, state_to, next_to, state_held, held, load_sem, store_sem):
    count = next_from.shape[0]

    def pairs(p):
        if p == count:
            return state_from, state_held, state_to
        return next_from.at[p], held.at[p], next_to.at[p]

    def load(p):
        source, here, _ = pairs(p)
        return pltpu.make_async_copy(source, here, load_sem.at[p])

    def store(p):
        _, here, target = pairs(p)
        return pltpu.make_async_copy(here, target, store_sem.at[p])

    for p in range(count + 1):
        load(p).start()
    for p in range(count + 1):
        load(p).wait()
        store(p).start()
    for p in range(count + 1):
        store(p).wait()


def shards(
    concentration,
    reaction_rates,
    coupling,
    profile,
    source_field,
    source_map,
    param_weight,
    sensitivity,
    courant,
):
    tiles, params = lax.axis_size("tile"), lax.axis_size("param")
    species = concentration.shape[0]
    layers = reaction_rates.shape[1]
    count = sensitivity.shape[0]
    sources = profile.shape[0]
    rows = species * layers
    f32, bf16 = jnp.float32, jnp.bfloat16
    vmem = pl.BlockSpec(memory_space=pltpu.VMEM)
    smem = pl.BlockSpec(memory_space=pltpu.SMEM)
    anywhere = pl.BlockSpec(memory_space=pl.ANY)
    halo = pltpu.VMEM((count, rows // 2, LANES), bf16)
    conc_halo = pltpu.VMEM((species // 2, LANES), bf16)
    dma = pltpu.SemaphoreType.DMA
    state, following = pl.pallas_call(
        partial(kernel, tiles, params),
        out_shape=(
            jax.ShapeDtypeStruct((species, LANES), f32),
            jax.ShapeDtypeStruct((count, rows, LANES), bf16),
        ),
        in_specs=[vmem] * 6 + [smem] * 2 + [anywhere],
        out_specs=(vmem, anywhere),
        scratch_shapes=[
            pltpu.VMEM((count, rows, LANES), bf16),
            pltpu.VMEM((count, rows, LANES), f32),
            halo,
            halo,
            halo,
            halo,
            halo,
            conc_halo,
            conc_halo,
            conc_halo,
            conc_halo,
            pltpu.VMEM((layers, species, LANES), f32),
            pltpu.VMEM((layers, species, LANES), WIRE),
            pltpu.VMEM((layers, species, LANES), f32),
            pltpu.VMEM((2 * ITERS + 1, layers, species, LANES), f32),
            pltpu.VMEM((sources, species, LANES), f32),
            pltpu.VMEM((GROUP, rows, LANES), f32),
            pltpu.VMEM((count, rows, LANES), bf16),
            dma((count,)),
            dma((count,)),
            dma((count,)),
            dma((count,)),
            dma((count,)),
            dma((count,)),
            dma((2,)),
            dma((2,)),
            dma((3,)),
            dma((3,)),
            dma((count,)),
            dma((count,)),
        ],
        compiler_params=pltpu.CompilerParams(
            collective_id=0, has_side_effects=True, vmem_limit_bytes=60 << 20
        ),
    )(
        concentration.reshape(species, LANES),
        reaction_rates.reshape(rows, LANES),
        coupling,
        profile,
        source_field.reshape(sources * layers, LANES),
        courant.reshape(4 * layers, LANES),
        source_map,
        param_weight,
        sensitivity.reshape(count, rows, LANES),
    )
    state, following = pl.pallas_call(
        hand_over,
        out_shape=(
            jax.ShapeDtypeStruct((species, LANES), f32),
            jax.ShapeDtypeStruct((count, rows, LANES), bf16),
        ),
        in_specs=[anywhere] * 2,
        out_specs=(anywhere,) * 2,
        scratch_shapes=[
            pltpu.VMEM((species, LANES), f32),
            pltpu.VMEM((count, rows, LANES), bf16),
            dma((count + 1,)),
            dma((count + 1,)),
        ],
        compiler_params=pltpu.CompilerParams(vmem_limit_bytes=60 << 20),
    )(state, following)
    return state.reshape(concentration.shape), following.reshape(sensitivity.shape)


def solution(mesh):
    placed = (
        P(None, "param", "tile"),
        P(None, None, "tile"),
        P(),
        P(),
        P(None, None, "tile"),
        P("param"),
        P("param"),
        P("param", None, None, "tile"),
        P(None, None, "tile"),
    )
    return jax.shard_map(
        shards,
        mesh=mesh,
        in_specs=placed,
        out_specs=(P(None, "param", "tile"), P("param", None, None, "tile")),
        check_vma=False,
    )
```

profile of v0, /device:TPU:6, one launch (start us, length us, event | category | flops | bytes accessed | tf_op | source)
XLA Modules:
  0.0 55.3 jit_solution(17611562272366280488)
XLA Ops:
  0.6 51.9 %shard_map.104 = (f32[160,128]{1,0:T(8,128)}, bf16[16,640,128]{2,1,0:T(8,128)(2,1)}) custom-call(f32[160,128]{1,0:T(8,128)} %bitcast.11, f32[640,128]{1,0:T(8,128)} %bitcast.10, bf16[160,160]{1,0:T(8,128)(2,1)} %coupling_ref.1, f32[16,160]{1,0:T(8,128)} %profile_ref.1, f32[64,128]{1,0:T(8,128)} %bitcast.12, f32[16,128]{1,0:T(8,128)} %bitcast.13, s32[16]{0:T(128)} %map_ref.1, ...), custom_call_target="tpu_custom_call" | custom-call | tf_op jit(solution)/shard_map/pallas_call | solution.py:491
  52.5 2.8 %shard_map.105 = (f32[160,128]{1,0:T(8,128)}, bf16[16,640,128]{2,1,0:T(8,128)(2,1)}) custom-call(f32[160,128]{1,0:T(8,128)} %get-tuple-element.6.state_from, bf16[16,640,128]{2,1,0:T(8,128)(2,1)} %get-tuple-element.7.next_from), custom_call_target="tpu_custom_call" | custom-call | tf_op jit(solution)/shard_map/pallas_call | solution.py:545
where the time goes:
time: 55.5 us; the launch traced here: 55.3 us
  Pallas kernels  54.7 us (99%)
  between operations  0.64 us (1%)
    pallas_call x1, Pallas kernels, shards(): pl.pallas_call(partial(kernel, tiles, params), out_shape=(jax.ShapeDtypeS...  51.9 us
    pallas_call x1, Pallas kernels, shards(): pl.pallas_call(hand_over, out_shape=(jax.ShapeDtypeStruct((species, LANES...  2.82 us

commit v1 on v0

--- a/solution.py
+++ b/solution.py
@@ -293,7 +293,7 @@
         pack(p)
         pl.when(jnp.logical_not(via))(lambda: issue(p))
 
-        @pl.when(p == count // 2)
+        @pl.when(p == READY + 1)
         def _():
             forward(0)
 

time: 55.5 us -> 56.2 us (1.013)
  Pallas kernels: 54.7 us -> 55.4 us
    pallas_call x1, Pallas kernels: 51.9 us -> 52.6 us  [shards(): pl.pallas_call(partial(kernel, tiles, params), out_shape=(jax.ShapeDtypeS...]
where the time goes in v1:
time: 56.2 us; the launch traced here: 56 us
  Pallas kernels  55.4 us (99%)
  between operations  0.64 us (1%)
    pallas_call x1, Pallas kernels, shards(): pl.pallas_call(partial(kernel, tiles, params), out_shape=(jax.ShapeDtypeS...  52.6 us
    pallas_call x1, Pallas kernels, shards(): pl.pallas_call(hand_over, out_shape=(jax.ShapeDtypeStruct((species, LANES...  2.82 us

profile of v1, /device:TPU:6, one launch (start us, length us, event | category | flops | bytes accessed | tf_op | source)
XLA Modules:
  0.0 56.0 jit_solution(11641364197429302706)
XLA Ops:
  0.6 52.6 %shard_map.104 = (f32[160,128]{1,0:T(8,128)}, bf16[16,640,128]{2,1,0:T(8,128)(2,1)}) custom-call(f32[160,128]{1,0:T(8,128)} %bitcast.11, f32[640,128]{1,0:T(8,128)} %bitcast.10, bf16[160,160]{1,0:T(8,128)(2,1)} %coupling_ref.1, f32[16,160]{1,0:T(8,128)} %profile_ref.1, f32[64,128]{1,0:T(8,128)} %bitcast.12, f32[16,128]{1,0:T(8,128)} %bitcast.13, s32[16]{0:T(128)} %map_ref.1, ...), custom_call_target="tpu_custom_call" | custom-call | tf_op jit(solution)/shard_map/pallas_call | solution.py:491
  53.2 2.8 %shard_map.105 = (f32[160,128]{1,0:T(8,128)}, bf16[16,640,128]{2,1,0:T(8,128)(2,1)}) custom-call(f32[160,128]{1,0:T(8,128)} %get-tuple-element.6.state_from, bf16[16,640,128]{2,1,0:T(8,128)(2,1)} %get-tuple-element.7.next_from), custom_call_target="tpu_custom_call" | custom-call | tf_op jit(solution)/shard_map/pallas_call | solution.py:545
